TPU v7x, 32 devices: a whole 2x2x4 slice. The times are simulated.
32 devices in a mesh: win: 2 (over x), chan: 16 (over z, y, core).
Axes of the slice: x: 2, y: 2, z: 4, core: 2. Of those that a mesh axis runs over, the one named last changes fastest.
Arguments:
- spectra: bfloat16 [8, 256, 2, 2048], P('win', 'chan')
- window_gain: float32 [8], P('win'), may hold values from 0.4 to 3
- dead_mask: int32 [8, 256], P('win', 'chan'), may hold values 0 or 1
- order: int32 [256], replicated, may hold values from 0 to 15
Outputs:
- stack: bfloat16 [256, 256, 2, 2048], P(None, 'chan', None, 'win')
- window_weight: float32 [8], P('win')
All inputs are finite; a program needn't handle non-finite values. No bound on the sum of `dead_mask` on one device may be relied on, other than what follows from the above.
Results may differ from a plain program's by a relative error of at most 0.0064.
Values may be sent and summed in bfloat16 or wider, within the bound.
A program may use at most 128 MiB of HBM per device.

v0:
```python
import jax
import jax.numpy as jnp
from jax import lax
from jax.sharding import PartitionSpec as P

ITERS = 2


def solve_stack(src_re, src_im, ch_re, ch_im, cells):
    f32 = jnp.float32
    bf16 = jnp.bfloat16
    corr_form = "ksf,kcf->scf"
    proj_form = "ksf,scf->kcf"
    row_axis = 1
    freq_axis = 1
    cross_axes = (1, 2)
    count = src_re.shape[0]
    a_square = jnp.sum(
        jnp.square(src_re.astype(f32)) + jnp.square(src_im.astype(f32)), axis=row_axis
    )
    b_square = jnp.sum(jnp.square(ch_re.astype(f32)) + jnp.square(ch_im.astype(f32)), axis=row_axis)
    energy = jnp.sum(a_square * b_square, axis=freq_axis)

    def product(form, left, right):
        return jnp.einsum(form, left, right, preferred_element_type=f32)

    def stack_of(weight):
        shaped = weight[:, None, None]
        w_re = (shaped * ch_re.astype(f32)).astype(bf16)
        w_im = (shaped * ch_im.astype(f32)).astype(bf16)
        total = jnp.sum(weight)
        gre = (product(corr_form, src_re, w_re) + product(corr_form, src_im, w_im)) / total
        gim = (product(corr_form, src_re, w_im) - product(corr_form, src_im, w_re)) / total
        return (gre.astype(bf16), gim.astype(bf16))

    weight = jnp.ones((count,), f32)
    for step in range(ITERS):
        gre, gim = stack_of(weight)
        p_re = product(proj_form, src_re, gre) - product(proj_form, src_im, gim)
        p_im = product(proj_form, src_re, gim) + product(proj_form, src_im, gre)
        cross = jnp.sum(ch_re.astype(f32) * p_re + ch_im.astype(f32) * p_im, axis=cross_axes)
        power = jnp.sum(jnp.square(gre.astype(f32)) + jnp.square(gim.astype(f32)))
        partial_misfit = energy - 2.0 * cross + power
        misfit = lax.psum(partial_misfit, ("win", "chan"))
        weight = 1.0 / jnp.sqrt(misfit / cells + 1e-06)
    gre, gim = stack_of(weight)
    return (gre, gim, weight)


def body(spectra, window_gain, dead_mask, order):
    f32 = jnp.float32
    bf16 = jnp.bfloat16
    scaled = (
        dead_mask.astype(f32)[:, :, None, None]
        * window_gain[:, None, None, None]
        * spectra.astype(f32)
    ).astype(bf16)
    sources = order.shape[0]
    per_dev = sources // lax.axis_size("chan")
    channels = spectra.shape[1]
    cells = sources * channels * lax.axis_size("chan") * spectra.shape[3]
    local = lax.all_to_all(scaled, "win", split_axis=3, concat_axis=0, tiled=True)
    first = lax.axis_index("chan") * per_dev
    mine = lax.dynamic_slice_in_dim(order, first, per_dev, 0)
    picked = jnp.take(local, mine, axis=1)
    gathered = lax.all_gather(picked, "chan", axis=1, tiled=True)
    gre, gim, weight = solve_stack(
        gathered[:, :, 0, :], gathered[:, :, 1, :], local[:, :, 0, :], local[:, :, 1, :], cells
    )
    stack = jnp.stack([gre, gim], axis=2)
    count = weight.shape[0]
    normed = weight * (count / jnp.sum(weight))
    first_window = lax.axis_index("win") * spectra.shape[0]
    window_weight = lax.dynamic_slice_in_dim(normed, first_window, spectra.shape[0], 0)
    return (stack, window_weight)


def solution(mesh):
    placed = (P("win", "chan", None, None), P("win"), P("win", "chan"), P())
    return jax.shard_map(
        body,
        mesh=mesh,
        in_specs=placed,
        out_specs=(P(None, "chan", None, "win"), P("win")),
        check_vma=False,
    )
```

profile of v0, /device:TPU:0, one launch (start us, length us, event | category | flops | bytes accessed | tf_op | source)
XLA Modules:
  0.0 486.6 jit_solution(12815705863949244203)
XLA Ops:
  25.7 8.1 %all-to-all-done = bf16[2,2,65536]{2,1,0:T(2,128)(2,1)S(1)} async-done(((bf16[2,2,65536]{2,1,0:T(2,128)(2,1)}), bf16[2,2,65536]{2,1,0:T(2,128)(2,1)S(1)}, u32[]{:S(2)}, u32[]{:S(2)}) %all-to-all-start) | async-done | bytes 524320 | tf_op jit(solution)/shard_map/all_to_all | solution.py:62
  53.3 72.2 %all-gather.2.cloned.1.call-done = bf16[8,256,2,1024]{3,0,2,1:T(8,128)(2,1)} async-done(((bf16[8,16,2,1024]{3,0,2,1:T(8,128)(2,1)}), bf16[8,256,2,1024]{3,0,2,1:T(8,128)(2,1)}) %all-gather.2.cloned.1.call-update) | async-done | bytes 8388624 | tf_op jit(solution)/shard_map/all_gather | solution.py:66
  138.8 10.1 %fusion.52 = f32[1024,16,256]{2,1,0:T(8,128)} fusion(bf16[8,256,1,1024]{1,0,3,2:T(8,128)(2,1)} %copy.28, bf16[8,16,2,1024]{1,0,3,2:T(8,128)(2,1)} %bitcast.154), kind=kOutput, calls=%fused_computation.73 | convolution fusion | flops 67108864 | bytes 23068672 | tf_op jit(solution)/shard_map/ksf,kcf->scf/dot_general | solution.py:25
  155.6 7.3 %copy.29 = bf16[8,256,1,1024]{1,0,3,2:T(8,128)(2,1)} copy(bf16[8,256,1,1024]{3,0,2,1:T(8,128)(2,1)} %get-tuple-element.13) | data formatting | bytes 8388608
  168.3 10.5 %multiply_convert_fusion.1 = bf16[1024,16,256]{2,1,0:T(8,128)(2,1)} fusion(f32[1024,16,256]{2,1,0:T(8,128)} %fusion.52, bf16[8,256,1,1024]{1,0,3,2:T(8,128)(2,1)S(1)} %copy-done.5, bf16[8,16,2,1024]{1,0,3,2:T(8,128)(2,1)} %bitcast.155), kind=kOutput, calls=%fused_computation.9 | convolution fusion | flops 79691776 | bytes 31457280 | tf_op jit(solution)/shard_map/ksf,kcf->scf/dot_general | solution.py:25
  178.8 7.7 %fusion.12 = f32[1024,16,8]{1,2,0:T(8,128)} fusion(bf16[1024,16,256]{2,1,0:T(8,128)(2,1)} %multiply_convert_fusion.1, bf16[8,256,1,1024]{1,0,3,2:T(8,128)(2,1)S(1)} %copy-done.5), kind=kOutput, calls=%fused_computation.22 | convolution fusion | flops 67108864 | bytes 13107200 | tf_op jit(solution)/shard_map/ksf,scf->kcf/dot_general | solution.py:25
  186.5 16.6 %add_reduce_fusion.1 = (f32[]{:T(128)}, bf16[1024,16,256]{2,1,0:T(8,128)(2,1)}) fusion(bf16[1024,16,256]{2,1,0:T(8,128)(2,1)} %multiply_convert_fusion.1, f32[1024,16,256]{2,1,0:T(8,128)} %fusion.49, bf16[8,256,1,1024]{1,0,3,2:T(8,128)(2,1)} %copy.29, bf16[8,16,2,1024]{1,0,3,2:T(8,128)(2,1)} %bitcast.156), kind=kOutput, calls=%fused_computation.7 | convolution fusion | flops 104857600 | bytes 39845892 | tf_op jit(solution)/shard_map/ksf,kcf->scf/dot_general | solution.py:25
  203.1 8.8 %fusion.8 = f32[1024,16,8]{1,2,0:T(8,128)} fusion(bf16[1024,16,256]{2,1,0:T(8,128)(2,1)} %get-tuple-element.19, bf16[8,256,1,1024]{1,0,3,2:T(8,128)(2,1)} %copy.28), kind=kOutput, calls=%fused_computation.18 | convolution fusion | flops 67108864 | bytes 13107200 | tf_op jit(solution)/shard_map/ksf,scf->kcf/dot_general | solution.py:25
  211.8 9.0 %fusion.10 = f32[1024,16,8]{1,2,0:T(8,128)} fusion(bf16[1024,16,256]{2,1,0:T(8,128)(2,1)} %get-tuple-element.19, bf16[8,256,1,1024]{1,0,3,2:T(8,128)(2,1)} %copy.29), kind=kOutput, calls=%fused_computation.20 | convolution fusion | flops 67108864 | bytes 13107200 | tf_op jit(solution)/shard_map/ksf,scf->kcf/dot_general | solution.py:25
  221.0 9.7 %fusion.21 = f32[8]{0:T(128)S(1)} fusion(f32[1024,16,8]{1,2,0:T(8,128)} %fusion.8, f32[1024,16,8]{1,2,0:T(8,128)} %fusion.12, f32[1024,16,8]{1,2,0:T(8,128)} %fusion.10, bf16[8,256,1,1024]{1,0,3,2:T(8,128)(2,1)S(1)} %copy-done.1, bf16[1024,16,256]{2,1,0:T(8,128)(2,1)} %multiply_convert_fusion.1, bf16[8,16,2,1024]{1,0,3,2:T(8,128)(2,1)} %bitcast.157), kind=kOutput, calls=%fused_computation.42 | convolution fusion | flops 68157432 | bytes 14680096 | tf_op jit(solution)/shard_map/ksf,scf->kcf/dot_general | solution.py:25
  231.3 38.8 %psum.14 = f32[8]{0:T(128)S(1)} all-reduce(f32[8]{0:T(128)S(1)} %subtract_add_fusion.1), channel_id=1, replica_groups=mesh['win'=2,'chan'=16] {'win','chan'}, use_global_device_ids=true, to_apply=%region_5.6 | all-reduce | flops 8 | bytes 64 | tf_op jit(solution)/shard_map/psum | solution.py:44
  270.7 10.2 %fusion.46 = f32[1024,16,256]{2,1,0:T(8,128)} fusion(bf16[8,256,1,1024]{1,0,3,2:T(8,128)(2,1)} %copy.28, f32[8]{0:T(128)S(1)} %get-tuple-element.17, bf16[8,16,2,1024]{1,0,3,2:T(8,128)(2,1)} %bitcast.158), kind=kOutput, calls=%fused_computation.67 | convolution fusion | flops 67502080 | bytes 23068704 | tf_op jit(solution)/shard_map/ksf,kcf->scf/dot_general | solution.py:25
  287.8 10.7 %divide_convert_fusion.3 = bf16[1024,16,256]{2,1,0:T(8,128)(2,1)} fusion(f32[1024,16,256]{2,1,0:T(8,128)} %fusion.46, f32[]{:T(128)} %get-tuple-element.16, bf16[8,256,1,1024]{1,0,3,2:T(8,128)(2,1)S(1)} %copy-done.6, f32[8]{0:T(128)S(1)} %get-tuple-element.17, bf16[8,16,2,1024]{1,0,3,2:T(8,128)(2,1)} %bitcast.159), kind=kOutput, calls=%fused_computation.6 | convolution fusion | flops 80084992 | bytes 31457824 | tf_op jit(solution)/shard_map/ksf,kcf->scf/dot_general | solution.py:25
  298.5 7.7 %fusion.4 = f32[1024,16,8]{1,2,0:T(8,128)} fusion(bf16[1024,16,256]{2,1,0:T(8,128)(2,1)} %divide_convert_fusion.3, bf16[8,256,1,1024]{1,0,3,2:T(8,128)(2,1)S(1)} %copy-done.6), kind=kOutput, calls=%fused_computation.14 | convolution fusion | flops 67108864 | bytes 13107200 | tf_op jit(solution)/shard_map/ksf,scf->kcf/dot_general | solution.py:25
  306.2 17.6 %add_reduce_fusion = (f32[]{:T(128)}, bf16[1024,16,256]{2,1,0:T(8,128)(2,1)}) fusion(bf16[1024,16,256]{2,1,0:T(8,128)(2,1)} %divide_convert_fusion.3, f32[]{:T(128)} %get-tuple-element.16, f32[1024,16,256]{2,1,0:T(8,128)} %fusion.43, bf16[8,256,1,1024]{1,0,3,2:T(8,128)(2,1)} %copy.29, f32[8]{0:T(128)S(1)} %get-tuple-element.17, ...), kind=kOutput, calls=%fused_computation.4 | convolution fusion | flops 105250816 | bytes 39846436 | tf_op jit(solution)/shard_map/ksf,kcf->scf/dot_general | solution.py:25
  323.7 8.8 %fusion = f32[1024,16,8]{1,2,0:T(8,128)} fusion(bf16[1024,16,256]{2,1,0:T(8,128)(2,1)} %get-tuple-element.21, bf16[8,256,1,1024]{1,0,3,2:T(8,128)(2,1)} %copy.28), kind=kOutput, calls=%fused_computation.10 | convolution fusion | flops 67108864 | bytes 13107200 | tf_op jit(solution)/shard_map/ksf,scf->kcf/dot_general | solution.py:25
  332.5 9.0 %fusion.2 = f32[1024,16,8]{1,2,0:T(8,128)} fusion(bf16[1024,16,256]{2,1,0:T(8,128)(2,1)} %get-tuple-element.21, bf16[8,256,1,1024]{1,0,3,2:T(8,128)(2,1)} %copy.29), kind=kOutput, calls=%fused_computation.12 | convolution fusion | flops 67108864 | bytes 13107200 | tf_op jit(solution)/shard_map/ksf,scf->kcf/dot_general | solution.py:25
  341.5 9.7 %fusion.24 = f32[8]{0:T(128)S(1)} fusion(f32[1024,16,8]{1,2,0:T(8,128)} %fusion, f32[1024,16,8]{1,2,0:T(8,128)} %fusion.4, f32[1024,16,8]{1,2,0:T(8,128)} %fusion.2, bf16[8,256,1,1024]{1,0,3,2:T(8,128)(2,1)S(1)} %copy-done.3, bf16[1024,16,256]{2,1,0:T(8,128)(2,1)} %divide_convert_fusion.3, bf16[8,16,2,1024]{1,0,3,2:T(8,128)(2,1)} %bitcast.161), kind=kOutput, calls=%fused_computation.45 | convolution fusion | flops 68157432 | bytes 14680096 | tf_op jit(solution)/shard_map/ksf,scf->kcf/dot_general | solution.py:25
  351.7 40.6 %psum.15 = f32[8]{0:T(128)S(1)} all-reduce(f32[8]{0:T(128)S(1)} %subtract_add_fusion), channel_id=1, replica_groups=mesh['win'=2,'chan'=16] {'win','chan'}, use_global_device_ids=true, to_apply=%region_9.10 | all-reduce | flops 8 | bytes 64 | tf_op jit(solution)/shard_map/psum | solution.py:44
  393.6 10.0 %fusion.38 = f32[1024,16,256]{2,1,0:T(8,128)} fusion(bf16[8,256,1,1024]{1,0,3,2:T(8,128)(2,1)} %copy.28, f32[8]{0:T(128)S(1)} %get-tuple-element.15, bf16[8,16,2,1024]{1,0,3,2:T(8,128)(2,1)} %bitcast.162), kind=kOutput, calls=%fused_computation.59 | convolution fusion | flops 67502080 | bytes 23068704 | tf_op jit(solution)/shard_map/ksf,kcf->scf/dot_general | solution.py:25
  410.5 11.8 %fusion.17 = bf16[256,16,1,1024]{0,1,3,2:T(8,128)(2,1)} fusion(f32[]{:T(128)} %fusion.71, f32[1024,16,256]{2,1,0:T(8,128)} %fusion.38, bf16[8,256,1,1024]{1,0,3,2:T(8,128)(2,1)S(1)} %copy-done.7, f32[8]{0:T(128)S(1)} %get-tuple-element.15, bf16[8,16,2,1024]{1,0,3,2:T(8,128)(2,1)S(1)} %bitcast.166), kind=kOutput, calls=%fused_computation.38 | convolution fusion | flops 80084992 | bytes 31457796 | tf_op jit(solution)/shard_map/ksf,kcf->scf/dot_general | solution.py:25
  422.4 11.8 %fusion.16 = bf16[256,16,1,1024]{0,1,3,2:T(8,128)(2,1)} fusion(f32[]{:T(128)} %fusion.71, f32[1024,16,256]{2,1,0:T(8,128)} %fusion.40, bf16[8,256,1,1024]{1,0,3,2:T(8,128)(2,1)S(1)} %copy-done.7, f32[8]{0:T(128)S(1)} %get-tuple-element.15, bf16[8,16,2,1024]{1,0,3,2:T(8,128)(2,1)S(1)} %bitcast.167), kind=kOutput, calls=%fused_computation.37 | convolution fusion | flops 80084992 | bytes 31457796 | tf_op jit(solution)/shard_map/ksf,kcf->scf/dot_general | solution.py:25
  434.2 13.7 %pad_maximum_fusion = bf16[256,16,2,1024]{0,1,3,2:T(8,128)(2,1)} fusion(bf16[256,16,1,1024]{0,1,3,2:T(8,128)(2,1)} %fusion.17, bf16[256,16,1,1024]{0,1,3,2:T(8,128)(2,1)} %fusion.16), kind=kLoop, calls=%fused_computation.1 | loop fusion | flops 8388608 | bytes 33554432 | tf_op jit(solution)/shard_map/stack | solution.py:70
  447.9 31.0 %copy.27 = bf16[256,16,2,1024]{3,2,1,0:T(2,128)(2,1)} copy(bf16[256,16,2,1024]{0,1,3,2:T(8,128)(2,1)} %pad_maximum_fusion) | data formatting | bytes 33554432
  (52 shorter events, 80.3 us)
Async XLA Ops:
  9.4 16.1 %copy-start.11 = (s32[256]{0:T(256)S(1)}, s32[256]{0:T(256)}, u32[]{:S(2)}) copy-start(s32[256]{0:T(256)} %param.7) | copy-start | bytes 3076
  20.8 12.9 %all-to-all-start = ((bf16[2,2,65536]{2,1,0:T(2,128)(2,1)}), bf16[2,2,65536]{2,1,0:T(2,128)(2,1)S(1)}, u32[]{:S(2)}, u32[]{:S(2)}) async-start(bf16[2,2,65536]{2,1,0:T(2,128)(2,1)} %reshape.25), calls=%async_computation | async-start | bytes 1048576 | tf_op jit(solution)/shard_map/all_to_all | solution.py:62
  25.0 100.5 %all-gather.2.cloned.1.call-start = ((), (), s32[]{:S(2)}) async-start(), calls=%async_computation.1 | async-start | bytes 8912896 | tf_op jit(solution)/shard_map/all_gather | solution.py:66
  138.8 10.1 %copy-start = (bf16[8,256,1,1024]{1,0,3,2:T(8,128)(2,1)S(1)}, bf16[8,256,1,1024]{1,0,3,2:T(8,128)(2,1)}, u32[]{:S(2)}) copy-start(bf16[8,256,1,1024]{1,0,3,2:T(8,128)(2,1)} %copy.28) | copy-start | bytes 12582916
  138.8 10.1 %copy-start.8 = (bf16[4,16,2,2,1024]{1,0,3,4,2:T(4,128)(2,1)S(1)}, bf16[4,16,2,2,1024]{1,0,3,4,2:T(4,128)(2,1)}, u32[]{:S(2)}) copy-start(bf16[4,16,2,2,1024]{1,0,3,4,2:T(4,128)(2,1)} %copy.23) | copy-start | bytes 1572868
  163.0 5.3 %copy-start.5 = (bf16[8,256,1,1024]{1,0,3,2:T(8,128)(2,1)S(1)}, bf16[8,256,1,1024]{1,0,3,2:T(8,128)(2,1)}, u32[]{:S(2)}) copy-start(bf16[8,256,1,1024]{1,0,3,2:T(8,128)(2,1)} %copy.29) | copy-start | bytes 12582916
  211.8 9.1 %copy-start.1 = (bf16[8,256,1,1024]{1,0,3,2:T(8,128)(2,1)S(1)}, bf16[8,256,1,1024]{1,0,3,2:T(8,128)(2,1)}, u32[]{:S(2)}) copy-start(bf16[8,256,1,1024]{1,0,3,2:T(8,128)(2,1)} %copy.28) | copy-start | bytes 12582916
  270.7 10.2 %copy-start.2 = (bf16[8,256,1,1024]{1,0,3,2:T(8,128)(2,1)S(1)}, bf16[8,256,1,1024]{1,0,3,2:T(8,128)(2,1)}, u32[]{:S(2)}) copy-start(bf16[8,256,1,1024]{1,0,3,2:T(8,128)(2,1)} %copy.28) | copy-start | bytes 12582916
  270.7 10.2 %copy-start.9 = (bf16[4,16,2,2,1024]{1,0,3,4,2:T(4,128)(2,1)S(1)}, bf16[4,16,2,2,1024]{1,0,3,4,2:T(4,128)(2,1)}, u32[]{:S(2)}) copy-start(bf16[4,16,2,2,1024]{1,0,3,4,2:T(4,128)(2,1)} %copy.23) | copy-start | bytes 1572868
  280.9 6.9 %copy-start.6 = (bf16[8,256,1,1024]{1,0,3,2:T(8,128)(2,1)S(1)}, bf16[8,256,1,1024]{1,0,3,2:T(8,128)(2,1)}, u32[]{:S(2)}) copy-start(bf16[8,256,1,1024]{1,0,3,2:T(8,128)(2,1)} %copy.29) | copy-start | bytes 12582916
  332.5 9.0 %copy-start.3 = (bf16[8,256,1,1024]{1,0,3,2:T(8,128)(2,1)S(1)}, bf16[8,256,1,1024]{1,0,3,2:T(8,128)(2,1)}, u32[]{:S(2)}) copy-start(bf16[8,256,1,1024]{1,0,3,2:T(8,128)(2,1)} %copy.28) | copy-start | bytes 12582916
  393.6 10.0 %copy-start.4 = (bf16[8,256,1,1024]{1,0,3,2:T(8,128)(2,1)S(1)}, bf16[8,256,1,1024]{1,0,3,2:T(8,128)(2,1)}, u32[]{:S(2)}) copy-start(bf16[8,256,1,1024]{1,0,3,2:T(8,128)(2,1)} %copy.28) | copy-start | bytes 12582916
  393.6 10.0 %copy-start.10 = (bf16[4,16,2,2,1024]{1,0,3,4,2:T(4,128)(2,1)S(1)}, bf16[4,16,2,2,1024]{1,0,3,4,2:T(4,128)(2,1)}, u32[]{:S(2)}) copy-start(bf16[4,16,2,2,1024]{1,0,3,4,2:T(4,128)(2,1)} %copy.23) | copy-start | bytes 1572868
  403.6 6.9 %copy-start.7 = (bf16[8,256,1,1024]{1,0,3,2:T(8,128)(2,1)S(1)}, bf16[8,256,1,1024]{1,0,3,2:T(8,128)(2,1)}, u32[]{:S(2)}) copy-start(bf16[8,256,1,1024]{1,0,3,2:T(8,128)(2,1)} %copy.29) | copy-start | bytes 12582916
Sparse Core Ops, SparseCore 0:
  50.0 75.4 all-gather.1
where the time goes:
time: 491 us; the launch traced here: 487 us
  matrix products  200 us (41%)
  waiting for transfers between devices  80.3 us (16%)
  blocking collectives  79.4 us (16%)
  local copies, waits for them, and re-layouts  78.8 us (16%)
  other arithmetic  28.3 us (6%)
  between operations  15.1 us (3%)
    dot_general x20, matrix products, product(): return jnp.einsum(form, left, right, preferred_element_type=f32)  200 us
    psum x2, blocking collectives, solve_stack(): misfit = lax.psum(partial_misfit, ('win', 'chan'))  79.4 us
    all_gather x1, waiting for transfers between devices, body(): gathered = lax.all_gather(picked, 'chan', axis=1, tiled=True)  72.2 us
    unnamed x29, local copies, waits for them, and re-layouts  56.4 us
    another operation x1, other arithmetic, body(): stack = jnp.stack([gre, gim], axis=2)  13.7 us
    all_to_all x2, local copies, waits for them, and re-layouts, body(): lax.all_to_all(scaled, 'win', split_axis=3, concat_axis=0, tiled=True)  10.5 us
  transfers between devices with their start and end apart: 2, of which 2 were waited for; matrix products, arithmetic and copies ran while one was open for 1% of the time, Pallas kernels for 0%

commit v1 on v0

--- a/solution.py
+++ b/solution.py
@@ -1,9 +1,16 @@
+import functools
+
 import jax
 import jax.numpy as jnp
 from jax import lax
+from jax.experimental import pallas as pl
+from jax.experimental.pallas import tpu as pltpu
 from jax.sharding import PartitionSpec as P
 
 ITERS = 2
+LANES = 128
+PART = 4
+MESH = pl.DeviceIdType.MESH
 
 
 def solve_stack(src_re, src_im, ch_re, ch_im, cells):
@@ -75,10 +82,470 @@
     return (stack, window_weight)
 
 
+def even_rows(shape):
+    return lax.rem(lax.broadcasted_iota(jnp.int32, shape, len(shape) - 2), 2) == 0
+
+
+def next_row(x):
+    return pltpu.roll(x, x.shape[0] - 1, 0)
+
+
+def prev_row(x):
+    return pltpu.roll(x, 1, 0)
+
+
+def swapped(x, even):
+    return jnp.where(even, next_row(x), prev_row(x))
+
+
+def gather_kernel(
+    cells,
+    scale_ref,
+    count_ref,
+    spectra_ref,
+    out_ref,
+    weight_ref,
+    held,
+    away,
+    grams,
+    lines,
+    sums,
+    halves,
+    out_sem,
+    x_sems,
+    up_sems,
+    down_sems,
+    y_sems,
+    pair_sems,
+    sum_sems,
+    half_sems,
+):
+    f32 = jnp.float32
+    bf16 = jnp.bfloat16
+    total = lax.axis_size("chan")
+    depth = total // 4
+    me = lax.axis_index("chan")
+    win = lax.axis_index("win")
+    core = lax.rem(me, 2)
+    row = lax.rem(me // 2, 2)
+    level = me // 4
+    windows, channels, rows = held.shape[1], held.shape[2], held.shape[3]
+    mine = windows // 2
+    step_windows = windows // PART
+    other = {"win": 1 - win}
+
+    def place(z, y):
+        return (z * 2 + y) * 2 + core
+
+    barrier = pltpu.get_barrier_semaphore()
+
+    @pl.loop(1, total)
+    def _(i):
+        pl.semaphore_signal(
+            barrier, inc=1, device_id={"chan": lax.rem(me + i, total)}, device_id_type=MESH
+        )
+
+    pl.semaphore_signal(barrier, inc=1, device_id=other, device_id_type=MESH)
+
+    for half in range(2):
+
+        @pl.when(win == half)
+        def _():
+            for k in range(mine):
+
+                @pl.loop(0, channels)
+                def _(c):
+                    scale = scale_ref[k, c]
+                    for part in range(2):
+                        value = spectra_ref[k, c, part * rows : (part + 1) * rows, :].astype(f32)
+                        value = (scale * value).astype(bf16)
+                        if part == half:
+                            held[me, half * mine + k, c] = value
+                        else:
+                            away[k, c] = value
+
+    pl.semaphore_wait(barrier, total)
+
+    def across(j):
+        start = pl.ds(j * step_windows, step_windows)
+        return pltpu.make_async_remote_copy(
+            src_ref=away.at[start],
+            dst_ref=held.at[me, pl.ds(win * mine + j * step_windows, step_windows)],
+            send_sem=x_sems.at[0, j],
+            recv_sem=x_sems.at[1, j],
+            device_id=other,
+            device_id_type=MESH,
+        )
+
+    for j in range(PART // 2):
+        across(j).start()
+
+    def piece(block, q):
+        return held.at[block, pl.ds(q * step_windows, step_windows)]
+
+    def send(block, q, sems, slot_out, slot_in, target):
+        return pltpu.make_async_remote_copy(
+            src_ref=piece(block, q),
+            dst_ref=piece(block, q),
+            send_sem=sems.at[0, slot_out, q],
+            recv_sem=sems.at[1, slot_in, q],
+            device_id={"chan": target},
+            device_id_type=MESH,
+        )
+
+    sibling = me + 1 - 2 * core
+
+    def up(block, q, t):
+        return send(block, q, up_sems, t, t + 1, lax.rem(me + 4, total))
+
+    def down(block, q, t):
+        return send(block, q, down_sems, t, t + 1, lax.rem(me + total - 4, total))
+
+    def cross(z, q):
+        return send(place(z, row), q, y_sems, z, z, place(level, 1 - row))
+
+    def pair(block, q):
+        return send(block, q, pair_sems, block // 2, block // 2, sibling)
+
+    def arrive(block, q, sems, slot):
+        send(block, q, sems, slot, slot, sibling).wait_recv()
+
+    def each(t, act):
+        if t == 0:
+            act(level, True, True)
+        else:
+
+            @pl.when(level - t >= 0)
+            def _():
+                act(level - t, True, False)
+
+            @pl.when(level + t < depth)
+            def _():
+                act(level + t, False, True)
+
+    def spread(t, q, act):
+        def one(z, rising, falling):
+            block = place(z, row)
+            if t > 0:
+                if act == "start":
+                    arrive(block, q, up_sems if rising else down_sems, t)
+            run = lambda copy: copy.start() if act == "start" else copy.wait_send()
+            if rising and t < depth - 1:
+
+                @pl.when(level < depth - 1)
+                def _():
+                    run(up(block, q, t))
+
+            if falling and t < depth - 1:
+
+                @pl.when(level > 0)
+                def _():
+                    run(down(block, q, t))
+
+            run(cross(z, q))
+            run(pair(block, q))
+
+        each(t, one)
+
+    def receive_cross(t, q, act):
+        def one(z, rising, falling):
+            block = place(z, 1 - row)
+            if act == "start":
+                arrive(block, q, y_sems, z)
+                pair(block, q).start()
+            else:
+                pair(block, q).wait_send()
+
+        each(t, one)
+
+    for t in range(depth + 1):
+
+        @pl.loop(0, PART)
+        def _(p):
+            q = lax.rem(p + win * (PART // 2), PART)
+            if t == 0:
+
+                @pl.when(p >= PART // 2)
+                def _():
+                    across(p - PART // 2).wait_recv()
+
+            if t < depth:
+                spread(t, q, "start")
+            if t > 0:
+                receive_cross(t - 1, q, "start")
+
+    @pl.loop(0, total // 2)
+    def _(i):
+        @pl.loop(0, PART)
+        def _(q):
+            block = i * 2 + 1 - core
+            arrive(block, q, pair_sems, i)
+
+    copy_out = pltpu.make_async_copy(held, out_ref, out_sem)
+    copy_out.start()
+
+    even = even_rows((rows, LANES))
+    for k in range(windows):
+        for j in range(k, windows):
+            for form in range(2):
+                grams[0, form, k * windows + j] = jnp.zeros((rows, LANES), f32)
+                grams[1, form, k * windows + j] = jnp.zeros((rows, LANES), f32)
+
+    @pl.loop(0, total + 1)
+    def _(i):
+        block = jnp.where(i == total, me, i)
+        which = jnp.where(i == total, 1, 0)
+        for k in range(windows):
+            zero = jnp.zeros((rows, LANES), f32)
+
+            def add(c, carry):
+                plain, turned = carry
+                x = held[block, k, c].astype(f32) * count_ref[i, c]
+                y = swapped(x, even)
+                new_plain, new_turned = [], []
+                for j in range(k, windows):
+                    z = held[block, j, c].astype(f32)
+                    new_plain.append(plain[j - k] + x * z)
+                    new_turned.append(turned[j - k] + y * z)
+                return tuple(new_plain), tuple(new_turned)
+
+            span = (zero,) * (windows - k)
+            plain, turned = lax.fori_loop(0, channels, add, (span, span))
+            for j in range(k, windows):
+                grams[which, 0, k * windows + j] += plain[j - k]
+                grams[which, 1, k * windows + j] += turned[j - k]
+
+    for k in range(windows):
+        for j in range(k, windows):
+            at = k * windows + j
+            value = jnp.zeros((rows, LANES), f32)
+            for form in range(2):
+                a, b = grams[0, form, at], grams[1, form, at]
+                sign = 1.0 if form == 0 else -1.0
+                value += (a + sign * next_row(a)) * (b + sign * next_row(b))
+            line = jnp.sum(jnp.where(even, value, 0.0), axis=0, keepdims=True)
+            lines[k, j : j + 1, :] = line
+            lines[j, k : k + 1, :] = line
+
+    lane = lax.broadcasted_iota(jnp.int32, (windows, LANES), 1)
+    sub = lax.broadcasted_iota(jnp.int32, (windows, LANES), 0)
+    part = jnp.zeros((windows, LANES), f32)
+    for k in range(windows):
+        part = jnp.where(lane == k, jnp.sum(lines[k], axis=1, keepdims=True), part)
+    sums[me] = part
+
+    def share(i):
+        target = lax.rem(me + i, total)
+        return pltpu.make_async_remote_copy(
+            src_ref=sums.at[me],
+            dst_ref=sums.at[me],
+            send_sem=sum_sems.at[0, target],
+            recv_sem=sum_sems.at[1, me],
+            device_id={"chan": target},
+            device_id_type=MESH,
+        )
+
+    @pl.loop(1, total)
+    def _(i):
+        share(i).start()
+
+    @pl.loop(1, total)
+    def _(i):
+        source = lax.rem(me + i, total)
+        pltpu.make_async_remote_copy(
+            src_ref=sums.at[source],
+            dst_ref=sums.at[source],
+            send_sem=sum_sems.at[0, source],
+            recv_sem=sum_sems.at[1, source],
+            device_id={"chan": source},
+            device_id_type=MESH,
+        ).wait_recv()
+
+    group = sums[0]
+    for i in range(1, total):
+        group = group + sums[i]
+    halves[0] = group
+    trade = pltpu.make_async_remote_copy(
+        src_ref=halves.at[0],
+        dst_ref=halves.at[1],
+        send_sem=half_sems.at[0],
+        recv_sem=half_sems.at[1],
+        device_id=other,
+        device_id_type=MESH,
+    )
+    trade.start()
+    trade.wait_recv()
+    table = halves[0] + halves[1]
+    diagonal = lane == sub
+    energy = jnp.sum(jnp.where(diagonal, table, 0.0), axis=0, keepdims=True)
+    live = lane[:1] < windows
+    weight = jnp.where(live, 1.0, 0.0)
+    for _ in range(ITERS):
+        column = jnp.sum(jnp.where(diagonal, weight, 0.0), axis=1, keepdims=True)
+        total_weight = jnp.sum(weight, axis=1, keepdims=True)
+        cross_row = jnp.sum(table * column, axis=0, keepdims=True) / total_weight
+        power = jnp.sum(weight * cross_row, axis=1, keepdims=True) / total_weight
+        misfit = energy - 2.0 * cross_row + power
+        weight = jnp.where(live, 1.0 / jnp.sqrt(misfit / cells + 1e-06), 0.0)
+    weight_ref[...] = weight / jnp.sum(weight, axis=1, keepdims=True)
+
+    for j in range(PART // 2):
+        across(j).wait_send()
+    for t in range(depth + 1):
+
+        @pl.loop(0, PART)
+        def _(q):
+            if t < depth:
+                spread(t, q, "end")
+            if t > 0:
+                receive_cross(t - 1, q, "end")
+
+    @pl.loop(1, total)
+    def _(i):
+        share(i).wait_send()
+
+    trade.wait_send()
+    copy_out.wait()
+
+
+def stack_kernel(pick_ref, weight_ref, source_ref, own_ref, out_ref, turned, first, second):
+    f32 = jnp.float32
+    bf16 = jnp.bfloat16
+    windows, channels, rows = turned.shape[0], turned.shape[1], turned.shape[2]
+    step = pl.program_id(0)
+    even = even_rows((rows, LANES))
+    per = out_ref.shape[0]
+
+    @pl.when(step == 0)
+    def _():
+        for k in range(windows):
+
+            @pl.loop(0, channels)
+            def _(c):
+                x = own_ref[0, k, c].astype(f32) * weight_ref[0, k]
+                first[c, k] = jnp.where(even, x, -prev_row(x)).astype(bf16)
+                second[c, k] = jnp.where(even, next_row(x), x).astype(bf16)
+
+    for k in range(windows):
+
+        @pl.loop(0, channels, unroll=4)
+        def _(c):
+            x = source_ref[0, k, c].astype(f32)
+            turned[k, c] = swapped(x, even).astype(bf16)
+
+    @pl.loop(0, per // 2)
+    def _(pair):
+        base = step * per + pair * 2
+        chosen = [pick_ref[base], pick_ref[base + 1]]
+        a = [[source_ref[0, k, i] for k in range(windows)] for i in chosen]
+        t = [[turned[k, i] for k in range(windows)] for i in chosen]
+
+        @pl.loop(0, channels, unroll=2)
+        def _(c):
+            b = [first[c, k] for k in range(windows)]
+            d = [second[c, k] for k in range(windows)]
+            for u in range(2):
+                terms = [a[u][k] * b[k] + t[u][k] * d[k] for k in range(windows)]
+                while len(terms) > 1:
+                    terms = [terms[i] + terms[i + 1] for i in range(0, len(terms), 2)]
+                out_ref[pair * 2 + u, c] = terms[0]
+
+
+def tiled(x):
+    lead, bins = x.shape[:-2], x.shape[-1]
+    x = x.reshape(*lead, 2, bins // LANES, LANES)
+    return jnp.swapaxes(x, -3, -2).reshape(*lead, bins // LANES * 2, LANES)
+
+
+def fast_body(spectra, window_gain, dead_mask, order):
+    f32 = jnp.float32
+    bf16 = jnp.bfloat16
+    total = lax.axis_size("chan")
+    mine, channels, _, bins = spectra.shape
+    windows = mine * 2
+    rows = bins // LANES
+    sources = order.shape[0]
+    per = sources // total
+    cells = float(sources * channels * total * bins)
+    scale = dead_mask.astype(f32) * window_gain[:, None]
+    hits = order.reshape(total, per, 1) == jnp.arange(channels, dtype=jnp.int32)
+    count = jnp.sum(hits.astype(f32), axis=1)
+    count = jnp.concatenate([count, jnp.ones((1, channels), f32)], axis=0)
+    smem = pl.BlockSpec(memory_space=pltpu.SMEM)
+    vmem = pl.BlockSpec(memory_space=pltpu.VMEM)
+    dma = pltpu.SemaphoreType.DMA
+    depth = total // 4
+    gathered, weight = pl.pallas_call(
+        functools.partial(gather_kernel, cells),
+        out_shape=(
+            jax.ShapeDtypeStruct((total, windows, channels, rows, LANES), bf16),
+            jax.ShapeDtypeStruct((1, LANES), f32),
+        ),
+        in_specs=[smem, smem, vmem],
+        out_specs=(pl.BlockSpec(memory_space=pl.ANY), vmem),
+        scratch_shapes=[
+            pltpu.VMEM((total, windows, channels, rows, LANES), bf16),
+            pltpu.VMEM((mine, channels, rows, LANES), bf16),
+            pltpu.VMEM((2, 2, windows * windows, rows, LANES), f32),
+            pltpu.VMEM((windows, windows, LANES), f32),
+            pltpu.VMEM((total, windows, LANES), f32),
+            pltpu.VMEM((2, windows, LANES), f32),
+            dma,
+            dma((2, PART // 2)),
+            dma((2, depth + 1, PART)),
+            dma((2, depth + 1, PART)),
+            dma((2, depth, PART)),
+            dma((2, total // 2, PART)),
+            dma((2, total)),
+            dma((2,)),
+        ],
+        compiler_params=pltpu.CompilerParams(
+            collective_id=0, has_side_effects=True, vmem_limit_bytes=40 * 2**20
+        ),
+        name="gather_sources",
+    )(scale, count, tiled(spectra))
+    pick = jnp.concatenate([order, lax.axis_index("chan")[None].astype(jnp.int32)])
+    block = (1, windows, channels, rows, LANES)
+    stack = pl.pallas_call(
+        stack_kernel,
+        out_shape=jax.ShapeDtypeStruct((sources, channels, rows, LANES), bf16),
+        grid_spec=pltpu.PrefetchScalarGridSpec(
+            num_scalar_prefetch=1,
+            grid=(total,),
+            in_specs=[
+                smem,
+                pl.BlockSpec(block, lambda i, pick: (i, 0, 0, 0, 0)),
+                pl.BlockSpec(block, lambda i, pick: (pick[sources], 0, 0, 0, 0)),
+            ],
+            out_specs=pl.BlockSpec((per, channels, rows, LANES), lambda i, pick: (i, 0, 0, 0)),
+            scratch_shapes=[
+                pltpu.VMEM((windows, channels, rows, LANES), bf16),
+                pltpu.VMEM((channels, windows, rows, LANES), bf16),
+                pltpu.VMEM((channels, windows, rows, LANES), bf16),
+            ],
+        ),
+        compiler_params=pltpu.CompilerParams(vmem_limit_bytes=40 * 2**20),
+        name="stack_sources",
+    )(pick, weight, gathered, gathered)
+    stack = stack.reshape(sources, channels, rows // 2, 2, LANES)
+    stack = jnp.swapaxes(stack, 2, 3).reshape(sources, channels, 2, bins // 2)
+    first = lax.axis_index("win") * mine
+    window_weight = windows * lax.dynamic_slice_in_dim(weight[0], first, mine, 0)
+    return (stack, window_weight)
+
+
 def solution(mesh):
     placed = (P("win", "chan", None, None), P("win"), P("win", "chan"), P())
+    wins, chans = mesh.shape["win"], mesh.shape["chan"]
+
+    def chosen(spectra, window_gain, dead_mask, order):
+        windows, _, _, bins = spectra.shape
+        fits = wins == 2 and windows * wins == 8 and chans % 4 == 0
+        fits = fits and bins % (16 * LANES) == 0 and order.shape[0] % (2 * chans) == 0
+        return (fast_body if fits else body)(spectra, window_gain, dead_mask, order)
+
     return jax.shard_map(
-        body,
+        chosen,
         mesh=mesh,
         in_specs=placed,
         out_specs=(P(None, "chan", None, "win"), P("win")),

time: 491 us -> 169 us (0.34)
  matrix products: 200 us -> 0 us
  Pallas kernels: 0 us -> 164 us
  waiting for transfers between devices: 80.3 us -> 0 us
  blocking collectives: 79.4 us -> 0 us
  local copies, waits for them, and re-layouts: 78.8 us -> 1.8 us
  other arithmetic: 28.3 us -> 2.15 us
  between operations: 15.1 us -> 0.67 us
    dot_general x20 -> x0, matrix products: 200 us -> none  [product(): return jnp.einsum(form, left, right, preferred_element_type=f32)]
    pallas_call x0 -> x2, Pallas kernels: none -> 164 us  [the longest x1 104 us: fast_body(): pl.pallas_call(functools.partial(gather_kernel, cells), out_shape=(jax.Sh...]
    psum x2 -> x0, blocking collectives: 79.4 us -> none  [solve_stack(): misfit = lax.psum(partial_misfit, ('win', 'chan'))]
    all_gather x1 -> x0, waiting for transfers between devices: 72.2 us -> none  [body(): gathered = lax.all_gather(picked, 'chan', axis=1, tiled=True)]
    unnamed x29 -> x2, local copies, waits for them, and re-layouts: 56.4 us -> 1.04 us
    another operation x1 -> x0, other arithmetic: 13.7 us -> none  [body(): stack = jnp.stack([gre, gim], axis=2)]
    all_to_all x2 -> x0, local copies, waits for them, and re-layouts: 10.5 us -> none  [body(): lax.all_to_all(scaled, 'win', split_axis=3, concat_axis=0, tiled=True)]
    reduce_sum x5 -> x1, other arithmetic: 10.1 us -> 0.12 us  [fast_body(): count = jnp.sum(hits.astype(f32), axis=1)]
  transfers between devices with their start and end apart: 2 -> 0, of which waited for: 2 -> 0; matrix products, arithmetic and copies ran while one was open for 1% -> 0% of each run, Pallas kernels for 0% -> 0%
where the time goes in v1:
time: 169 us; the launch traced here: 168 us
  Pallas kernels  164 us (97%)
  other arithmetic  2.15 us (1%)
  local copies, waits for them, and re-layouts  1.8 us (1%)
    pallas_call x1, Pallas kernels, fast_body(): pl.pallas_call(functools.partial(gather_kernel, cells), out_shape=(jax.Sh...  104 us
    pallas_call x1, Pallas kernels, fast_body(): pl.pallas_call(stack_kernel, out_shape=jax.ShapeDtypeStruct((sources, cha...  60 us

profile of v1, /device:TPU:0, one launch (start us, length us, event | category | flops | bytes accessed | tf_op | source)
XLA Modules:
  0.0 168.4 jit_solution(4865251757198255747)
XLA Ops:
  0.6 0.7 pad_add_fusion.pick_ref
  1.3 0.8 convert_multiply_fusion.scale_ref
  2.1 0.8 eq.15
  2.8 0.1 convert_reduce_fusion
  3.0 0.0 copy-start
  3.0 1.0 copy-done
  4.0 103.8 %gather_sources.1 = (bf16[16,8,16,16,128]{4,3,2,1,0:T(8,128)(2,1)S(1)}, f32[1,128]{1,0:T(1,128)S(1)}) custom-call(f32[4,16]{1,0:T(4,128)S(1)} %convert_multiply_fusion.scale_ref, f32[17,16]{1,0:T(8,128)S(1)} %concatenate.7.count_ref, bf16[4,16,32,128]{3,2,1,0:T(8,128)(2,1)S(1)} %bitcast.13), custom_call_target="tpu_custom_call" | custom-call | tf_op jit(solution)/shard_map/gather_sources/pallas_call | solution.py:478
  107.8 0.6 multiply_bitcast_fusion
  108.4 60.0 %stack_sources.1 = bf16[256,16,16,128]{3,2,1,0:T(8,128)(2,1)} custom-call(s32[257]{0:T(512)S(1)} %pad_add_fusion.pick_ref, f32[1,128]{1,0:T(1,128)S(1)} %get-tuple-element.4.weight_ref, bf16[16,8,16,16,128]{4,3,2,1,0:T(8,128)(2,1)S(1)} %get-tuple-element.5.source_ref.own_ref, bf16[16,8,16,16,128]{4,3,2,1,0:T(8,128)(2,1)S(1)} %get-tuple-element.5.source_ref.own_ref), custom_call_target="tpu_custom_call" | custom-call | tf_op jit(solution)/shard_map/stack_sources/pallas_call | solution.py:509
  (1 shorter events, 0.0 us)
Async XLA Ops:
  3.0 1.0 copy-start

commit v2 on v1

--- a/solution.py
+++ b/solution.py
@@ -111,7 +111,7 @@
     lines,
     sums,
     halves,
-    out_sem,
+    out_sems,
     x_sems,
     up_sems,
     down_sems,
@@ -258,32 +258,6 @@
 
         each(t, one)
 
-    for t in range(depth + 1):
-
-        @pl.loop(0, PART)
-        def _(p):
-            q = lax.rem(p + win * (PART // 2), PART)
-            if t == 0:
-
-                @pl.when(p >= PART // 2)
-                def _():
-                    across(p - PART // 2).wait_recv()
-
-            if t < depth:
-                spread(t, q, "start")
-            if t > 0:
-                receive_cross(t - 1, q, "start")
-
-    @pl.loop(0, total // 2)
-    def _(i):
-        @pl.loop(0, PART)
-        def _(q):
-            block = i * 2 + 1 - core
-            arrive(block, q, pair_sems, i)
-
-    copy_out = pltpu.make_async_copy(held, out_ref, out_sem)
-    copy_out.start()
-
     even = even_rows((rows, LANES))
     for k in range(windows):
         for j in range(k, windows):
@@ -291,29 +265,78 @@
                 grams[0, form, k * windows + j] = jnp.zeros((rows, LANES), f32)
                 grams[1, form, k * windows + j] = jnp.zeros((rows, LANES), f32)
 
-    @pl.loop(0, total + 1)
-    def _(i):
-        block = jnp.where(i == total, me, i)
-        which = jnp.where(i == total, 1, 0)
+    def gram(which, block, factors):
         for k in range(windows):
             zero = jnp.zeros((rows, LANES), f32)
 
             def add(c, carry):
                 plain, turned = carry
-                x = held[block, k, c].astype(f32) * count_ref[i, c]
+                x = held[block, k, c].astype(f32) * count_ref[factors, c]
                 y = swapped(x, even)
                 new_plain, new_turned = [], []
                 for j in range(k, windows):
                     z = held[block, j, c].astype(f32)
                     new_plain.append(plain[j - k] + x * z)
-                    new_turned.append(turned[j - k] + y * z)
+                    if j > k:
+                        new_turned.append(turned[j - k - 1] + y * z)
                 return tuple(new_plain), tuple(new_turned)
 
             span = (zero,) * (windows - k)
-            plain, turned = lax.fori_loop(0, channels, add, (span, span))
+            plain, turned = lax.fori_loop(0, channels, add, (span, span[1:]), unroll=4)
             for j in range(k, windows):
                 grams[which, 0, k * windows + j] += plain[j - k]
-                grams[which, 1, k * windows + j] += turned[j - k]
+                if j > k:
+                    grams[which, 1, k * windows + j] += turned[j - k - 1]
+
+    def copy_out(block):
+        return pltpu.make_async_copy(held.at[block], out_ref.at[block], out_sems.at[block])
+
+    def settle(t, y, theirs):
+        def one(z, rising, falling):
+            mate = place(z, y)
+            block = mate + theirs * (1 - 2 * core)
+
+            @pl.when(theirs == 1)
+            def _():
+                for q in range(PART):
+                    arrive(block, q, pair_sems, block // 2)
+
+            copy_out(block).start()
+            gram(0, block, block)
+
+        if t >= 0:
+            each(t, one)
+
+    for t in range(depth + 1):
+
+        @pl.loop(0, PART)
+        def _(p):
+            q = lax.rem(p + win * (PART // 2), PART)
+            if t == 0:
+
+                @pl.when(p >= PART // 2)
+                def _():
+                    across(p - PART // 2).wait_recv()
+
+            if t < depth:
+                spread(t, q, "start")
+            if t > 0:
+                receive_cross(t - 1, q, "start")
+
+                @pl.when(p < 2)
+                def _():
+                    settle(t - 1, row, p)
+
+                @pl.when(p >= 2)
+                def _():
+                    settle(t - 2, 1 - row, p - 2)
+
+        if t == 0:
+            gram(1, me, total)
+
+    @pl.loop(0, 2)
+    def _(p):
+        settle(depth - 1, 1 - row, p)
 
     for k in range(windows):
         for j in range(k, windows):
@@ -405,7 +428,10 @@
         share(i).wait_send()
 
     trade.wait_send()
-    copy_out.wait()
+
+    @pl.loop(0, total)
+    def _(i):
+        copy_out(i).wait()
 
 
 def stack_kernel(pick_ref, weight_ref, source_ref, own_ref, out_ref, turned, first, second):
@@ -423,8 +449,9 @@
             @pl.loop(0, channels)
             def _(c):
                 x = own_ref[0, k, c].astype(f32) * weight_ref[0, k]
-                first[c, k] = jnp.where(even, x, -prev_row(x)).astype(bf16)
-                second[c, k] = jnp.where(even, next_row(x), x).astype(bf16)
+                x = x.astype(bf16).astype(f32)
+                first[c, k] = jnp.where(even, x, -prev_row(x))
+                second[c, k] = jnp.where(even, next_row(x), x)
 
     for k in range(windows):
 
@@ -433,22 +460,19 @@
             x = source_ref[0, k, c].astype(f32)
             turned[k, c] = swapped(x, even).astype(bf16)
 
-    @pl.loop(0, per // 2)
-    def _(pair):
-        base = step * per + pair * 2
-        chosen = [pick_ref[base], pick_ref[base + 1]]
-        a = [[source_ref[0, k, i] for k in range(windows)] for i in chosen]
-        t = [[turned[k, i] for k in range(windows)] for i in chosen]
-
-        @pl.loop(0, channels, unroll=2)
+    @pl.loop(0, per)
+    def _(s):
+        i = pick_ref[step * per + s]
+        a = [source_ref[0, k, i].astype(f32) for k in range(windows)]
+        t = [turned[k, i].astype(f32) for k in range(windows)]
+
+        @pl.loop(0, channels, unroll=16)
         def _(c):
-            b = [first[c, k] for k in range(windows)]
-            d = [second[c, k] for k in range(windows)]
-            for u in range(2):
-                terms = [a[u][k] * b[k] + t[u][k] * d[k] for k in range(windows)]
-                while len(terms) > 1:
-                    terms = [terms[i] + terms[i + 1] for i in range(0, len(terms), 2)]
-                out_ref[pair * 2 + u, c] = terms[0]
+            value = None
+            for k in range(windows):
+                term = a[k] * first[c, k] + t[k] * second[c, k]
+                value = term if value is None else value + term
+            out_ref[s, c] = value.astype(bf16)
 
 
 def tiled(x):
@@ -490,7 +514,7 @@
             pltpu.VMEM((windows, windows, LANES), f32),
             pltpu.VMEM((total, windows, LANES), f32),
             pltpu.VMEM((2, windows, LANES), f32),
-            dma,
+            dma((total,)),
             dma((2, PART // 2)),
             dma((2, depth + 1, PART)),
             dma((2, depth + 1, PART)),
@@ -520,8 +544,8 @@
             out_specs=pl.BlockSpec((per, channels, rows, LANES), lambda i, pick: (i, 0, 0, 0)),
             scratch_shapes=[
                 pltpu.VMEM((windows, channels, rows, LANES), bf16),
-                pltpu.VMEM((channels, windows, rows, LANES), bf16),
-                pltpu.VMEM((channels, windows, rows, LANES), bf16),
+                pltpu.VMEM((channels, windows, rows, LANES), f32),
+                pltpu.VMEM((channels, windows, rows, LANES), f32),
             ],
         ),
         compiler_params=pltpu.CompilerParams(vmem_limit_bytes=40 * 2**20),

time: 169 us -> 121 us (0.72)
  Pallas kernels: 164 us -> 116 us
    pallas_call x1, Pallas kernels: 104 us -> 69.2 us  [fast_body(): pl.pallas_call(functools.partial(gather_kernel, cells), out_shape=(jax.Sh...]
    pallas_call x1, Pallas kernels: 60 us -> 47.1 us  [fast_body(): pl.pallas_call(stack_kernel, out_shape=jax.ShapeDtypeStruct((sources, cha...]
where the time goes in v2:
time: 121 us
  Pallas kernels  116 us (96%)
  other arithmetic  2.15 us (2%)
  local copies, waits for them, and re-layouts  1.8 us (1%)
    pallas_call x1, Pallas kernels, fast_body(): pl.pallas_call(functools.partial(gather_kernel, cells), out_shape=(jax.Sh...  69.2 us
    pallas_call x1, Pallas kernels, fast_body(): pl.pallas_call(stack_kernel, out_shape=jax.ShapeDtypeStruct((sources, cha...  47.1 us

profile of v2, /device:TPU:0, one launch (start us, length us, event | category | flops | bytes accessed | tf_op | source)
XLA Modules:
  0.0 121.0 jit_solution(5061131107433535030)
XLA Ops:
  0.6 0.7 pad_add_fusion.pick_ref
  1.3 0.8 convert_multiply_fusion.scale_ref
  2.1 0.8 eq.15
  2.8 0.1 convert_reduce_fusion
  3.0 0.0 copy-start
  3.0 1.0 copy-done
  4.0 69.2 %gather_sources.1 = (bf16[16,8,16,16,128]{4,3,2,1,0:T(8,128)(2,1)S(1)}, f32[1,128]{1,0:T(1,128)S(1)}) custom-call(f32[4,16]{1,0:T(4,128)S(1)} %convert_multiply_fusion.scale_ref, f32[17,16]{1,0:T(8,128)S(1)} %concatenate.7.count_ref, bf16[4,16,32,128]{3,2,1,0:T(8,128)(2,1)S(1)} %bitcast.13), custom_call_target="tpu_custom_call" | custom-call | tf_op jit(solution)/shard_map/gather_sources/pallas_call | solution.py:502
  73.2 0.6 multiply_bitcast_fusion
  73.8 47.1 %stack_sources.1 = bf16[256,16,16,128]{3,2,1,0:T(8,128)(2,1)} custom-call(s32[257]{0:T(512)S(1)} %pad_add_fusion.pick_ref, f32[1,128]{1,0:T(1,128)S(1)} %get-tuple-element.4.weight_ref, bf16[16,8,16,16,128]{4,3,2,1,0:T(8,128)(2,1)S(1)} %get-tuple-element.5.source_ref.own_ref, bf16[16,8,16,16,128]{4,3,2,1,0:T(8,128)(2,1)S(1)} %get-tuple-element.5.source_ref.own_ref), custom_call_target="tpu_custom_call" | custom-call | tf_op jit(solution)/shard_map/stack_sources/pallas_call | solution.py:533
  (1 shorter events, 0.0 us)
Async XLA Ops:
  3.0 1.0 copy-start

commit v3 on v2

--- a/solution.py
+++ b/solution.py
@@ -116,6 +116,8 @@
     up_sems,
     down_sems,
     y_sems,
+    rise_sems,
+    fall_sems,
     pair_sems,
     sum_sems,
     half_sems,
@@ -147,23 +149,24 @@
 
     pl.semaphore_signal(barrier, inc=1, device_id=other, device_id_type=MESH)
 
-    for half in range(2):
-
-        @pl.when(win == half)
-        def _():
-            for k in range(mine):
-
-                @pl.loop(0, channels)
+    def prepare(kept):
+        for half in range(2):
+
+            @pl.when(win == half)
+            def _():
+                part = half if kept else 1 - half
+
+                @pl.loop(0, channels, unroll=4)
                 def _(c):
-                    scale = scale_ref[k, c]
-                    for part in range(2):
+                    for k in range(mine):
                         value = spectra_ref[k, c, part * rows : (part + 1) * rows, :].astype(f32)
-                        value = (scale * value).astype(bf16)
-                        if part == half:
+                        value = (scale_ref[k, c] * value).astype(bf16)
+                        if kept:
                             held[me, half * mine + k, c] = value
                         else:
                             away[k, c] = value
 
+    prepare(False)
     pl.semaphore_wait(barrier, total)
 
     def across(j):
@@ -179,6 +182,7 @@
 
     for j in range(PART // 2):
         across(j).start()
+    prepare(True)
 
     def piece(block, q):
         return held.at[block, pl.ds(q * step_windows, step_windows)]
@@ -201,6 +205,12 @@
     def down(block, q, t):
         return send(block, q, down_sems, t, t + 1, lax.rem(me + total - 4, total))
 
+    def rise(block, q, t):
+        return send(block, q, rise_sems, t, t + 1, lax.rem(me + 4, total))
+
+    def fall(block, q, t):
+        return send(block, q, fall_sems, t, t + 1, lax.rem(me + total - 4, total))
+
     def cross(z, q):
         return send(place(z, row), q, y_sems, z, z, place(level, 1 - row))
 
@@ -223,7 +233,7 @@
             def _():
                 act(level + t, False, True)
 
-    def spread(t, q, act):
+    def spread(t, q, late, act):
         def one(z, rising, falling):
             block = place(z, row)
             if t > 0:
@@ -242,19 +252,48 @@
                 def _():
                     run(down(block, q, t))
 
-            run(cross(z, q))
+            if t == 0:
+                run(cross(z, q))
+            else:
+
+                @pl.when(jnp.logical_not(late))
+                def _():
+                    run(cross(z, q))
+
             run(pair(block, q))
 
         each(t, one)
 
-    def receive_cross(t, q, act):
+    def receive_cross(t, q, late, act):
         def one(z, rising, falling):
             block = place(z, 1 - row)
+            run = lambda copy: copy.start() if act == "start" else copy.wait_send()
             if act == "start":
-                arrive(block, q, y_sems, z)
-                pair(block, q).start()
-            else:
-                pair(block, q).wait_send()
+                if t == 0:
+                    arrive(block, q, y_sems, z)
+                else:
+
+                    @pl.when(late)
+                    def _():
+                        arrive(block, q, rise_sems if rising else fall_sems, t)
+
+                    @pl.when(jnp.logical_not(late))
+                    def _():
+                        arrive(block, q, y_sems, z)
+
+            if rising and t < depth - 1:
+
+                @pl.when(jnp.logical_and(late, level < depth - 1))
+                def _():
+                    run(rise(block, q, t))
+
+            if falling and t < depth - 1:
+
+                @pl.when(jnp.logical_and(late, level > 0))
+                def _():
+                    run(fall(block, q, t))
+
+            run(pair(block, q))
 
         each(t, one)
 
@@ -319,9 +358,9 @@
                     across(p - PART // 2).wait_recv()
 
             if t < depth:
-                spread(t, q, "start")
+                spread(t, q, p == PART - 1, "start")
             if t > 0:
-                receive_cross(t - 1, q, "start")
+                receive_cross(t - 1, q, p == PART - 1, "start")
 
                 @pl.when(p < 2)
                 def _():
@@ -417,11 +456,12 @@
     for t in range(depth + 1):
 
         @pl.loop(0, PART)
-        def _(q):
+        def _(p):
+            q = lax.rem(p + win * (PART // 2), PART)
             if t < depth:
-                spread(t, q, "end")
+                spread(t, q, p == PART - 1, "end")
             if t > 0:
-                receive_cross(t - 1, q, "end")
+                receive_cross(t - 1, q, p == PART - 1, "end")
 
     @pl.loop(1, total)
     def _(i):
@@ -455,7 +495,7 @@
 
     for k in range(windows):
 
-        @pl.loop(0, channels, unroll=4)
+        @pl.loop(0, channels, unroll=16)
         def _(c):
             x = source_ref[0, k, c].astype(f32)
             turned[k, c] = swapped(x, even).astype(bf16)
@@ -519,6 +559,8 @@
             dma((2, depth + 1, PART)),
             dma((2, depth + 1, PART)),
             dma((2, depth, PART)),
+            dma((2, depth + 1, PART)),
+            dma((2, depth + 1, PART)),
             dma((2, total // 2, PART)),
             dma((2, total)),
             dma((2,)),

time: 121 us -> 118 us (0.975)
  Pallas kernels: 116 us -> 113 us
    pallas_call x1, Pallas kernels: 47.1 us -> 45.3 us  [fast_body(): pl.pallas_call(stack_kernel, out_shape=jax.ShapeDtypeStruct((sources, cha...]
    pallas_call x1, Pallas kernels: 69.2 us -> 67.9 us  [fast_body(): pl.pallas_call(functools.partial(gather_kernel, cells), out_shape=(jax.Sh...]
where the time goes in v3:
time: 118 us
  Pallas kernels  113 us (96%)
  other arithmetic  2.15 us (2%)
  local copies, waits for them, and re-layouts  1.8 us (2%)
    pallas_call x1, Pallas kernels, fast_body(): pl.pallas_call(functools.partial(gather_kernel, cells), out_shape=(jax.Sh...  67.9 us
    pallas_call x1, Pallas kernels, fast_body(): pl.pallas_call(stack_kernel, out_shape=jax.ShapeDtypeStruct((sources, cha...  45.3 us

profile of v3, /device:TPU:0, one launch (start us, length us, event | category | flops | bytes accessed | tf_op | source)
XLA Modules:
  0.0 117.8 jit_solution(5245180983898488863)
XLA Ops:
  0.6 0.7 pad_add_fusion.pick_ref
  1.3 0.8 convert_multiply_fusion.scale_ref
  2.1 0.8 eq.15
  2.8 0.1 convert_reduce_fusion
  3.0 0.0 copy-start
  3.0 1.0 copy-done
  4.0 67.9 %gather_sources.1 = (bf16[16,8,16,16,128]{4,3,2,1,0:T(8,128)(2,1)S(1)}, f32[1,128]{1,0:T(1,128)S(1)}) custom-call(f32[4,16]{1,0:T(4,128)S(1)} %convert_multiply_fusion.scale_ref, f32[17,16]{1,0:T(8,128)S(1)} %concatenate.7.count_ref, bf16[4,16,32,128]{3,2,1,0:T(8,128)(2,1)S(1)} %bitcast.13), custom_call_target="tpu_custom_call" | custom-call | tf_op jit(solution)/shard_map/gather_sources/pallas_call | solution.py:542
  72.0 0.6 multiply_bitcast_fusion
  72.5 45.3 %stack_sources.1 = bf16[256,16,16,128]{3,2,1,0:T(8,128)(2,1)} custom-call(s32[257]{0:T(512)S(1)} %pad_add_fusion.pick_ref, f32[1,128]{1,0:T(1,128)S(1)} %get-tuple-element.4.weight_ref, bf16[16,8,16,16,128]{4,3,2,1,0:T(8,128)(2,1)S(1)} %get-tuple-element.5.source_ref.own_ref, bf16[16,8,16,16,128]{4,3,2,1,0:T(8,128)(2,1)S(1)} %get-tuple-element.5.source_ref.own_ref), custom_call_target="tpu_custom_call" | custom-call | tf_op jit(solution)/shard_map/stack_sources/pallas_call | solution.py:575
  (1 shorter events, 0.0 us)
Async XLA Ops:
  3.0 1.0 copy-start
